TPU v7x, 32 devices: a whole 2x2x4 slice. The times are simulated.
32 devices in a mesh: segment: 16 (over z, x, core), band: 2 (over y).
Axes of the slice: x: 2, y: 2, z: 4, core: 2. Of those that a mesh axis runs over, the one named last changes fastest.
Arguments:
- first_input: bfloat16 [16, 16, 128, 256], P('segment', 'band'), may hold values from -6 to 6
- stashed: bfloat16 [16, 2, 16, 128, 256], P('segment', None, 'band'), may hold values from -6 to 6
- first_grad: bfloat16 [16, 16, 128, 256], P('segment', 'band'), may hold values from -6 to 6
- weight_now: bfloat16 [16, 3, 3, 256, 256], P('segment'), may hold values from -5 to 5
- weight_old: bfloat16 [16, 3, 3, 256, 256], P('segment'), may hold values from -5 to 5
- momentum: float32 [16, 3, 3, 256, 256], P('segment'), may hold values from -6 to 6
- slot_plan: int32 [2, 16], P(None, 'segment'), may hold values from 0 to 1
- next_input: bfloat16 [16, 128, 256], P('band'), may hold values from -6 to 6
- next_grad: bfloat16 [16, 128, 256], P('band'), may hold values from -6 to 6
Outputs:
- act_out: bfloat16 [16, 16, 128, 256], P('segment', 'band')
- grad_out: bfloat16 [16, 16, 128, 256], P('segment', 'band')
- weight_now_out: bfloat16 [16, 3, 3, 256, 256], P('segment')
- weight_old_out: bfloat16 [16, 3, 3, 256, 256], P('segment')
- momentum_out: float32 [16, 3, 3, 256, 256], P('segment')
All inputs are finite; a program needn't handle non-finite values.
Results may differ from a plain program's by a relative error of at most 0.009.
Values may be sent and summed in bfloat16 or wider, within the bound.
No kernel may reach another device: no remote copies, remote signals or barrier semaphores. Data moves between devices by JAX's collectives and lax.ppermute only.
A program may use at most 128 MiB of HBM per device.

v0:
```python
import math

import jax
import jax.numpy as jnp
from jax import lax
from jax.sharding import PartitionSpec as P

C = 256


def padded_2(block, sides, width):
    for axis, dim in sides:
        count = lax.axis_size(axis)
        forward = [(i, i + 1) for i in range(count - 1)]
        backward = [(target, source) for source, target in forward]
        low = lax.ppermute(
            lax.slice_in_dim(block, block.shape[dim] - width, None, axis=dim), axis, forward
        )
        high = lax.ppermute(lax.slice_in_dim(block, 0, width, axis=dim), axis, backward)
        block = jnp.concatenate([low, block, high], axis=dim)
    return block


def passed_along(array, axis, by):
    length = lax.axis_size(axis)
    pairs = [(i, i + by) for i in range(length) if 0 <= i + by < length]
    return lax.ppermute(array, axis, pairs)


def row_patches(extended, rows):
    wcol = extended.shape[1]
    padded = jnp.pad(extended, ((0, 0), (1, 1), (0, 0)))
    taps = [padded[ky : ky + rows, kx : kx + wcol, :] for ky in range(3) for kx in range(3)]
    return jnp.concatenate(taps, axis=2).reshape(rows * wcol, -1)


def silu_slope(value):
    sig = jax.nn.sigmoid(value)
    return sig * (1.0 + value * (1.0 - sig))


def forward_part(x_in, flat_now, factor):
    rows, wcol = (x_in.shape[0], x_in.shape[1])
    ext = padded_2(x_in, (("band", 0),), 1)
    pre = jnp.dot(row_patches(ext, rows), flat_now, preferred_element_type=jnp.float32) * factor
    return jax.nn.silu(pre).astype(jnp.bfloat16).reshape(rows, wcol, C)


def backward_part(chosen, grad, w_old, factor):
    rows, wcol = (chosen.shape[0], chosen.shape[1])
    flat_old = w_old.reshape(9 * C, C)
    flip_old = w_old[::-1, ::-1].transpose(0, 1, 3, 2).reshape(9 * C, C)
    ext = padded_2(chosen, (("band", 0),), 1)
    patches = row_patches(ext, rows)
    back = jnp.dot(patches, flat_old, preferred_element_type=jnp.float32) * factor
    slope_grad = (grad.reshape(-1, C) * silu_slope(back)).astype(jnp.bfloat16)
    slope_ext = padded_2(slope_grad.reshape(rows, wcol, C), (("band", 0),), 1)
    kgrad = (
        lax.dot_general(
            patches, slope_grad, (((0,), (0,)), ((), ())), preferred_element_type=jnp.float32
        )
        * factor
    )
    in_grad = (
        jnp.dot(row_patches(slope_ext, rows), flip_old, preferred_element_type=jnp.float32) * factor
    )
    return (in_grad.astype(jnp.bfloat16).reshape(rows, wcol, C), kgrad)


def update_part(kgrad, w_now, moment):
    flat_now = w_now.reshape(9 * C, C).astype(jnp.float32)
    total = lax.psum(kgrad.astype(jnp.bfloat16), "band").astype(jnp.float32)
    new_moment = 0.9 * moment + total
    new_flat = (flat_now - 0.05 * new_moment).astype(jnp.bfloat16)
    return (new_flat.reshape(3, 3, C, C), new_moment)


def body(
    first_input,
    stashed,
    first_grad,
    weight_now,
    weight_old,
    momentum,
    slot_plan,
    next_input,
    next_grad,
):
    factor = 1.0 / math.sqrt(9 * C)
    segment_pos = lax.axis_index("segment")
    last_pos = lax.axis_size("segment") - 1
    x_in = first_input[0]
    stash = stashed[0]
    grad = first_grad[0]
    w_now = weight_now[0]
    w_old = weight_old[0]
    moment = momentum[0].reshape(9 * C, C)
    slots = slot_plan[:, 0]
    for tick in range(2):
        if tick == 1:
            arrived = passed_along(out_acts, "segment", 1)
            x_in = jnp.where(segment_pos == 0, next_input, arrived)
            returned = passed_along(in_grad, "segment", -1)
            grad = jnp.where(segment_pos == last_pos, next_grad, returned)
        out_acts = forward_part(x_in, w_now.reshape(9 * C, C), factor)
        chosen = lax.dynamic_index_in_dim(stash, slots[tick], 0, keepdims=False)
        in_grad, kgrad = backward_part(chosen, grad, w_old, factor)
        stash = lax.dynamic_update_index_in_dim(stash, x_in, slots[tick], 0)
        new_weight, moment = update_part(kgrad, w_now, moment)
        w_old = w_now
        w_now = new_weight
    return (out_acts[None], in_grad[None], w_now[None], w_old[None], moment.reshape(1, 3, 3, C, C))


def solution(mesh):
    placed = (
        P("segment", "band", None, None),
        P("segment", None, "band", None, None),
        P("segment", "band", None, None),
        P("segment", None, None, None, None),
        P("segment", None, None, None, None),
        P("segment", None, None, None, None),
        P(None, "segment"),
        P("band", None, None),
        P("band", None, None),
    )
    return jax.shard_map(
        body,
        mesh=mesh,
        in_specs=placed,
        out_specs=(
            P("segment", "band", None, None),
            P("segment", "band", None, None),
            P("segment", None, None, None, None),
            P("segment", None, None, None, None),
            P("segment", None, None, None, None),
        ),
        check_vma=False,
    )
```

profile of v0, /device:TPU:27, one launch (start us, length us, event | category | flops | bytes accessed | tf_op | source)
XLA Modules:
  0.0 185.4 jit_solution(11654778727878078919)
XLA Ops:
  8.5 1.3 fusion.20
  12.4 3.1 %collective-permute-start.5 = (bf16[1,128,256]{2,1,0:T(8,128)(2,1)}, bf16[1,128,256]{2,1,0:T(8,128)(2,1)S(1)}, u32[]{:S(2)}, u32[]{:S(2)}) collective-permute-start(bf16[1,128,256]{2,1,0:T(8,128)(2,1)} %get-tuple-element.12), channel_id=1, source_target_pairs={{0,1},{2,3},{4,5},{6,7},{8,9},{10,11},{12,13},{14,15},{16,17},{18,... | collective-permute-start | bytes 196616 | tf_op jit(solution)/shard_map/ppermute | solution.py:16
  21.2 4.6 %collective-permute-start.10 = (bf16[1,128,256]{2,1,0:T(8,128)(2,1)}, bf16[1,128,256]{2,1,0:T(8,128)(2,1)S(1)}, u32[]{:S(2)}, u32[]{:S(2)}) collective-permute-start(bf16[1,128,256]{2,1,0:T(8,128)(2,1)} %get-tuple-element.10), channel_id=1, source_target_pairs={{0,1},{2,3},{4,5},{6,7},{8,9},{10,11},{12,13},{14,15},{16,17},{18,... | collective-permute-start | bytes 196616 | tf_op jit(solution)/shard_map/ppermute | solution.py:16
  27.7 4.0 %collective-permute-start = (bf16[1,128,256]{2,1,0:T(8,128)(2,1)}, bf16[1,128,256]{2,1,0:T(8,128)(2,1)S(1)}, u32[]{:S(2)}, u32[]{:S(2)}) collective-permute-start(bf16[1,128,256]{2,1,0:T(8,128)(2,1)} %get-tuple-element.60), channel_id=1, source_target_pairs={{0,1},{2,3},{4,5},{6,7},{8,9},{10,11},{12,13},{14,15},{16,17},{18,... | collective-permute-start | bytes 196616 | tf_op jit(solution)/shard_map/ppermute | solution.py:16
  31.8 1.8 copy.14
  34.7 1.6 copy.15
  37.4 3.3 %broadcast_multiply_fusion = f32[1,3,3,256,256]{4,3,2,1,0:T(8,128)} fusion(f32[1,3,3,256,256]{4,3,2,1,0:T(8,128)} %param.14), kind=kLoop, calls=%fused_computation.19 | loop fusion | flops 589824 | bytes 4718592 | tf_op jit(solution)/shard_map/mul | solution.py:73
  45.0 1.6 fusion.6
  46.6 2.5 %fusion = bf16[2304,256]{1,0:T(8,128)(2,1)} fusion(bf16[1024,2304]{1,0:T(8,128)(2,1)S(1)} %constant_dynamic-update-slice_fusion.10, bf16[1024,256]{1,0:T(8,128)(2,1)S(1)} %fusion.6), kind=kOutput, calls=%fused_computation.2 | convolution fusion | flops 1209139200 | bytes 6422528 | tf_op jit(solution)/shard_map/dot_general | solution.py:59
  49.1 4.0 %collective-permute-start.7 = (bf16[1,128,256]{2,1,0:T(8,128)(2,1)S(1)}, bf16[1,128,256]{2,1,0:T(8,128)(2,1)S(1)}, u32[]{:S(2)}, u32[]{:S(2)}) collective-permute-start(bf16[1,128,256]{2,1,0:T(8,128)(2,1)S(1)} %get-tuple-element.50), channel_id=1, source_target_pairs={{0,1},{2,3},{4,5},{6,7},{8,9},{10,11},{12,13},{14,15},{16,17},{18,... | collective-permute-start | bytes 196616 | tf_op jit(solution)/shard_map/ppermute | solution.py:16
  57.2 1.4 multiply_convert_fusion.1
  61.5 3.0 %collective-permute-done.2 = bf16[8,128,256]{2,1,0:T(8,128)(2,1)S(1)} collective-permute-done((bf16[8,128,256]{2,1,0:T(8,128)(2,1)S(1)}, bf16[8,128,256]{2,1,0:T(8,128)(2,1)S(1)}, u32[]{:S(2)}, u32[]{:S(2)}) %collective-permute-start.2) | collective-permute-done | bytes 524320 | tf_op jit(solution)/shard_map/ppermute | solution.py:27
  64.6 4.3 %collective-permute-start.3 = (bf16[1,128,256]{2,1,0:T(8,128)(2,1)S(1)}, bf16[1,128,256]{2,1,0:T(8,128)(2,1)S(1)}, u32[]{:S(2)}, u32[]{:S(2)}) collective-permute-start(bf16[1,128,256]{2,1,0:T(8,128)(2,1)S(1)} %get-tuple-element.56), channel_id=1, source_target_pairs={{0,1},{2,3},{4,5},{6,7},{8,9},{10,11},{12,13},{14,15},{16,17},{18,... | collective-permute-start | bytes 196616 | tf_op jit(solution)/shard_map/ppermute | solution.py:16
  70.2 1.4 fusion.3
  71.6 9.7 %collective-permute-start.9 = (bf16[8,128,256]{2,1,0:T(8,128)(2,1)S(1)}, bf16[8,128,256]{2,1,0:T(8,128)(2,1)S(1)}, u32[]{:S(2)}, u32[]{:S(2)}) collective-permute-start(bf16[8,128,256]{2,1,0:T(8,128)(2,1)S(1)} %bitcast.185), channel_id=1, source_target_pairs={{2,0},{4,2},{6,4},{8,6},{10,8},{12,10},{14,12},{16,14},{18,16},{20... | collective-permute-start | bytes 1572872 | tf_op jit(solution)/shard_map/ppermute | solution.py:27
  82.7 1.6 copy-done.19
  84.3 1.6 fusion.5
  86.0 2.5 %fusion.1 = bf16[2304,256]{1,0:T(8,128)(2,1)} fusion(bf16[1024,2304]{1,0:T(8,128)(2,1)S(1)} %constant_dynamic-update-slice_fusion.28, bf16[1024,256]{1,0:T(8,128)(2,1)S(1)} %fusion.5), kind=kOutput, calls=%fused_computation.3 | convolution fusion | flops 1209139200 | bytes 6422528 | tf_op jit(solution)/shard_map/dot_general | solution.py:59
  88.5 4.3 %collective-permute-start.12 = (bf16[1,128,256]{2,1,0:T(8,128)(2,1)S(1)}, bf16[1,128,256]{2,1,0:T(8,128)(2,1)S(1)}, u32[]{:S(2)}, u32[]{:S(2)}) collective-permute-start(bf16[1,128,256]{2,1,0:T(8,128)(2,1)S(1)} %get-tuple-element.46), channel_id=1, source_target_pairs={{0,1},{2,3},{4,5},{6,7},{8,9},{10,11},{12,13},{14,15},{16,17},{18,... | collective-permute-start | bytes 196616 | tf_op jit(solution)/shard_map/ppermute | solution.py:16
  95.0 2.7 %collective-permute-done.13 = bf16[1,128,256]{2,1,0:T(8,128)(2,1)S(1)} collective-permute-done((bf16[1,128,256]{2,1,0:T(8,128)(2,1)S(1)}, bf16[1,128,256]{2,1,0:T(8,128)(2,1)S(1)}, u32[]{:S(2)}, u32[]{:S(2)}) %collective-permute-start.13) | collective-permute-done | bytes 65568 | tf_op jit(solution)/shard_map/ppermute | solution.py:19
  99.6 2.2 %fusion.4 = bf16[1024,256]{1,0:T(8,128)(2,1)} fusion(bf16[1024,2304]{1,0:T(8,128)(2,1)S(1)} %constant_dynamic-update-slice_fusion.37, bf16[2304,256]{1,0:T(8,128)(2,1)S(1)} %bitcast.178), kind=kOutput, calls=%fused_computation.18 | convolution fusion | flops 1208483840 | bytes 6422528 | tf_op jit(solution)/shard_map/dot_general | solution.py:65
  101.8 67.3 %all-reduce.9.cloned.1.call-done = (bf16[2304,256]{1,0:T(8,128)(2,1)}, bf16[2304,256]{1,0:T(8,128)(2,1)}) async-done(((bf16[2304,256]{1,0:T(8,128)(2,1)}, bf16[2304,256]{1,0:T(8,128)(2,1)}), (bf16[2304,256]{1,0:T(8,128)(2,1)}, bf16[2304,256]{1,0:T(8,128)(2,1)})) %all-reduce.9.cloned.1.call-update) | async-done | bytes 2359312 | tf_op jit(solution)/shard_map/psum | solution.py:72
  169.1 4.4 %subtract_convert_fusion = (bf16[2304,256]{1,0:T(8,128)(2,1)}, f32[2304,256]{1,0:T(8,128)}, bf16[2304,256]{1,0:T(8,128)(2,1)S(1)}) fusion(bf16[2304,256]{1,0:T(8,128)(2,1)} %get-tuple-element.6, bf16[2304,256]{1,0:T(8,128)(2,1)} %get-tuple-element.5, f32[1,3,3,256,256]{4,3,2,1,0:T(8,128)S(1)} %copy-done.1, bf16[1,3,3,256,256]{4,3,2,1,0:T(8,128)(2,1)S(1)} %copy-done.2), kind=kLoop, calls=%fused_computation.5 | loop fusion | flops 7667712 | bytes 10616832 | tf_op jit(solution)/shard_map/convert_element_type | solution.py:74
  173.5 5.0 %multiply_convert_fusion = bf16[1024,256]{1,0:T(8,128)(2,1)} fusion(bf16[1024,2304]{1,0:T(8,128)(2,1)} %bitcast.182, bf16[2304,256]{1,0:T(8,128)(2,1)S(1)} %get-tuple-element.9), kind=kOutput, calls=%fused_computation.24 | convolution fusion | flops 1209532416 | bytes 6422528 | tf_op jit(solution)/shard_map/dot_general | solution.py:45
  (148 shorter events, 27.2 us)
Async XLA Ops:
  7.2 13.3 %copy-start = (bf16[1,8,128,256]{3,2,1,0:T(8,128)(2,1)S(1)}, bf16[1,8,128,256]{3,2,1,0:T(8,128)(2,1)}, u32[]{:S(2)}) copy-start(bf16[1,8,128,256]{3,2,1,0:T(8,128)(2,1)} %param.9) | copy-start | bytes 1572868
  7.2 161.9 %all-reduce.9.cloned.1.call-start = ((), (), s32[]{:S(2)}) async-start(), calls=%async_computation | async-start | bytes 4718592 | tf_op jit(solution)/shard_map/psum | solution.py:72
  12.4 28.3 %collective-permute-start.5 = (bf16[1,128,256]{2,1,0:T(8,128)(2,1)}, bf16[1,128,256]{2,1,0:T(8,128)(2,1)S(1)}, u32[]{:S(2)}, u32[]{:S(2)}) collective-permute-start(bf16[1,128,256]{2,1,0:T(8,128)(2,1)} %get-tuple-element.12), channel_id=1, source_target_pairs={{0,1},{2,3},{4,5},{6,7},{8,9},{10,11},{12,13},{14,15},{16,17},{18,... | collective-permute-start | bytes 196616 | tf_op jit(solution)/shard_map/ppermute | solution.py:16
  15.6 26.5 %collective-permute-start.6 = (bf16[1,128,256]{2,1,0:T(8,128)(2,1)}, bf16[1,128,256]{2,1,0:T(8,128)(2,1)}, u32[]{:S(2)}, u32[]{:S(2)}) collective-permute-start(bf16[1,128,256]{2,1,0:T(8,128)(2,1)} %get-tuple-element.13), channel_id=1, source_target_pairs={{1,0},{3,2},{5,4},{7,6},{9,8},{11,10},{13,12},{15,14},{17,16},{19,... | collective-permute-start | bytes 196616 | tf_op jit(solution)/shard_map/ppermute | solution.py:19
  21.2 31.9 %collective-permute-start.10 = (bf16[1,128,256]{2,1,0:T(8,128)(2,1)}, bf16[1,128,256]{2,1,0:T(8,128)(2,1)S(1)}, u32[]{:S(2)}, u32[]{:S(2)}) collective-permute-start(bf16[1,128,256]{2,1,0:T(8,128)(2,1)} %get-tuple-element.10), channel_id=1, source_target_pairs={{0,1},{2,3},{4,5},{6,7},{8,9},{10,11},{12,13},{14,15},{16,17},{18,... | collective-permute-start | bytes 196616 | tf_op jit(solution)/shard_map/ppermute | solution.py:16
  25.8 28.6 %collective-permute-start.11 = (bf16[1,128,256]{2,1,0:T(8,128)(2,1)}, bf16[1,128,256]{2,1,0:T(8,128)(2,1)S(1)}, u32[]{:S(2)}, u32[]{:S(2)}) collective-permute-start(bf16[1,128,256]{2,1,0:T(8,128)(2,1)} %get-tuple-element.11), channel_id=1, source_target_pairs={{1,0},{3,2},{5,4},{7,6},{9,8},{11,10},{13,12},{15,14},{17,16},{19,... | collective-permute-start | bytes 196616 | tf_op jit(solution)/shard_map/ppermute | solution.py:19
  27.7 27.3 %collective-permute-start = (bf16[1,128,256]{2,1,0:T(8,128)(2,1)}, bf16[1,128,256]{2,1,0:T(8,128)(2,1)S(1)}, u32[]{:S(2)}, u32[]{:S(2)}) collective-permute-start(bf16[1,128,256]{2,1,0:T(8,128)(2,1)} %get-tuple-element.60), channel_id=1, source_target_pairs={{0,1},{2,3},{4,5},{6,7},{8,9},{10,11},{12,13},{14,15},{16,17},{18,... | collective-permute-start | bytes 196616 | tf_op jit(solution)/shard_map/ppermute | solution.py:16
  31.8 22.6 %copy-start.3 = (bf16[8,128,256]{2,1,0:T(8,128)(2,1)}, bf16[8,128,256]{2,1,0:T(8,128)(2,1)S(1)}, u32[]{:S(2)}) copy-start(bf16[8,128,256]{2,1,0:T(8,128)(2,1)S(1)} %fusion.37) | copy-start | bytes 1572868
  37.4 3.4 %copy-start.18 = (bf16[1,128,256]{2,1,0:T(8,128)(2,1)S(1)}, bf16[1,128,256]{2,1,0:T(8,128)(2,1)}, u32[]{:S(2)}) copy-start(bf16[1,128,256]{2,1,0:T(8,128)(2,1)} %get-tuple-element.61) | copy-start | bytes 196612
  37.4 4.7 %copy-start.5 = (bf16[8,128,256]{2,1,0:T(8,128)(2,1)S(1)}, bf16[8,128,256]{2,1,0:T(8,128)(2,1)}, u32[]{:S(2)}) copy-start(bf16[8,128,256]{2,1,0:T(8,128)(2,1)} %fusion.38) | copy-start | bytes 1572868
  40.8 14.3 %collective-permute-start.1 = (bf16[1,128,256]{2,1,0:T(8,128)(2,1)S(1)}, bf16[1,128,256]{2,1,0:T(8,128)(2,1)S(1)}, u32[]{:S(2)}, u32[]{:S(2)}) collective-permute-start(bf16[1,128,256]{2,1,0:T(8,128)(2,1)S(1)} %copy-done.18), channel_id=1, source_target_pairs={{1,0},{3,2},{5,4},{7,6},{9,8},{11,10},{13,12},{15,14},{17,16},{19,... | collective-permute-start | bytes 196616 | tf_op jit(solution)/shard_map/ppermute | solution.py:19
  49.1 11.3 %collective-permute-start.7 = (bf16[1,128,256]{2,1,0:T(8,128)(2,1)S(1)}, bf16[1,128,256]{2,1,0:T(8,128)(2,1)S(1)}, u32[]{:S(2)}, u32[]{:S(2)}) collective-permute-start(bf16[1,128,256]{2,1,0:T(8,128)(2,1)S(1)} %get-tuple-element.50), channel_id=1, source_target_pairs={{0,1},{2,3},{4,5},{6,7},{8,9},{10,11},{12,13},{14,15},{16,17},{18,... | collective-permute-start | bytes 196616 | tf_op jit(solution)/shard_map/ppermute | solution.py:16
  53.1 7.3 %collective-permute-start.8 = (bf16[1,128,256]{2,1,0:T(8,128)(2,1)S(1)}, bf16[1,128,256]{2,1,0:T(8,128)(2,1)S(1)}, u32[]{:S(2)}, u32[]{:S(2)}) collective-permute-start(bf16[1,128,256]{2,1,0:T(8,128)(2,1)S(1)} %get-tuple-element.51), channel_id=1, source_target_pairs={{1,0},{3,2},{5,4},{7,6},{9,8},{11,10},{13,12},{15,14},{17,16},{19,... | collective-permute-start | bytes 196616 | tf_op jit(solution)/shard_map/ppermute | solution.py:19
  58.6 5.9 %collective-permute-start.2 = (bf16[8,128,256]{2,1,0:T(8,128)(2,1)S(1)}, bf16[8,128,256]{2,1,0:T(8,128)(2,1)S(1)}, u32[]{:S(2)}, u32[]{:S(2)}) collective-permute-start(bf16[8,128,256]{2,1,0:T(8,128)(2,1)S(1)} %bitcast.184), channel_id=1, source_target_pairs={{0,2},{2,4},{4,6},{6,8},{8,10},{10,12},{12,14},{14,16},{16,18},{18... | collective-permute-start | bytes 1572872 | tf_op jit(solution)/shard_map/ppermute | solution.py:27
  61.1 3.5 %copy-start.11 = (bf16[8,128,256]{2,1,0:T(8,128)(2,1)S(1)}, bf16[8,128,256]{2,1,0:T(8,128)(2,1)}, u32[]{:S(2)}) copy-start(bf16[8,128,256]{2,1,0:T(8,128)(2,1)} %param.16) | copy-start | bytes 1572868
  61.2 9.0 %copy-start.9 = (bf16[3,3,256,256]{2,3,1,0:T(8,128)(2,1)S(1)}, bf16[3,3,256,256]{2,3,1,0:T(8,128)(2,1)}, u32[]{:S(2)}) copy-start(bf16[3,3,256,256]{2,3,1,0:T(8,128)(2,1)} %rev.6) | copy-start | bytes 3538948
  64.6 16.7 %collective-permute-start.3 = (bf16[1,128,256]{2,1,0:T(8,128)(2,1)S(1)}, bf16[1,128,256]{2,1,0:T(8,128)(2,1)S(1)}, u32[]{:S(2)}, u32[]{:S(2)}) collective-permute-start(bf16[1,128,256]{2,1,0:T(8,128)(2,1)S(1)} %get-tuple-element.56), channel_id=1, source_target_pairs={{0,1},{2,3},{4,5},{6,7},{8,9},{10,11},{12,13},{14,15},{16,17},{18,... | collective-permute-start | bytes 196616 | tf_op jit(solution)/shard_map/ppermute | solution.py:16
  68.9 12.5 %collective-permute-start.4 = (bf16[1,128,256]{2,1,0:T(8,128)(2,1)S(1)}, bf16[1,128,256]{2,1,0:T(8,128)(2,1)S(1)}, u32[]{:S(2)}, u32[]{:S(2)}) collective-permute-start(bf16[1,128,256]{2,1,0:T(8,128)(2,1)S(1)} %get-tuple-element.57), channel_id=1, source_target_pairs={{1,0},{3,2},{5,4},{7,6},{9,8},{11,10},{13,12},{15,14},{17,16},{19,... | collective-permute-start | bytes 196616 | tf_op jit(solution)/shard_map/ppermute | solution.py:19
  71.6 12.7 %copy-start.12 = (bf16[8,128,256]{2,1,0:T(8,128)(2,1)S(1)}, bf16[8,128,256]{2,1,0:T(8,128)(2,1)}, u32[]{:S(2)}) copy-start(bf16[8,128,256]{2,1,0:T(8,128)(2,1)} %param.17) | copy-start | bytes 1572868
  71.6 11.0 %collective-permute-start.9 = (bf16[8,128,256]{2,1,0:T(8,128)(2,1)S(1)}, bf16[8,128,256]{2,1,0:T(8,128)(2,1)S(1)}, u32[]{:S(2)}, u32[]{:S(2)}) collective-permute-start(bf16[8,128,256]{2,1,0:T(8,128)(2,1)S(1)} %bitcast.185), channel_id=1, source_target_pairs={{2,0},{4,2},{6,4},{8,6},{10,8},{12,10},{14,12},{16,14},{18,16},{20... | collective-permute-start | bytes 1572872 | tf_op jit(solution)/shard_map/ppermute | solution.py:27
  88.5 6.6 %collective-permute-start.12 = (bf16[1,128,256]{2,1,0:T(8,128)(2,1)S(1)}, bf16[1,128,256]{2,1,0:T(8,128)(2,1)S(1)}, u32[]{:S(2)}, u32[]{:S(2)}) collective-permute-start(bf16[1,128,256]{2,1,0:T(8,128)(2,1)S(1)} %get-tuple-element.46), channel_id=1, source_target_pairs={{0,1},{2,3},{4,5},{6,7},{8,9},{10,11},{12,13},{14,15},{16,17},{18,... | collective-permute-start | bytes 196616 | tf_op jit(solution)/shard_map/ppermute | solution.py:16
  92.7 5.0 %collective-permute-start.13 = (bf16[1,128,256]{2,1,0:T(8,128)(2,1)S(1)}, bf16[1,128,256]{2,1,0:T(8,128)(2,1)S(1)}, u32[]{:S(2)}, u32[]{:S(2)}) collective-permute-start(bf16[1,128,256]{2,1,0:T(8,128)(2,1)S(1)} %get-tuple-element.47), channel_id=1, source_target_pairs={{1,0},{3,2},{5,4},{7,6},{9,8},{11,10},{13,12},{15,14},{17,16},{19,... | collective-permute-start | bytes 196616 | tf_op jit(solution)/shard_map/ppermute | solution.py:19
  99.6 69.5 %copy-start.1 = (f32[1,3,3,256,256]{4,3,2,1,0:T(8,128)S(1)}, f32[1,3,3,256,256]{4,3,2,1,0:T(8,128)}, u32[]{:S(2)}) copy-start(f32[1,3,3,256,256]{4,3,2,1,0:T(8,128)} %broadcast_multiply_fusion) | copy-start | bytes 7077892
  173.5 5.0 %copy-start.10 = (bf16[2304,256]{1,0:T(8,128)(2,1)}, bf16[2304,256]{1,0:T(8,128)(2,1)S(1)}, u32[]{:S(2)}) copy-start(bf16[2304,256]{1,0:T(8,128)(2,1)S(1)} %get-tuple-element.9) | copy-start | bytes 3538948
  (12 other events, 21.3 us)
Sparse Core Ops, SparseCore 0:
  94.2 74.8 all-reduce.8
where the time goes:
time: 188 us; the launch traced here: 185 us
  waiting for transfers between devices  73.6 us (39%)
  starting transfers between devices  43 us (23%)
  local copies, waits for them, and re-layouts  19.4 us (10%)
  between operations  19 us (10%)
  matrix products  18.2 us (10%)
  other arithmetic  12.2 us (6%)
    psum x1, waiting for transfers between devices, update_part(): total = lax.psum(kgrad.astype(jnp.bfloat16), 'band').astype(jnp.float32)  67.3 us
    ppermute x6, starting transfers between devices, padded_2(): lax.ppermute(lax.slice_in_dim(block, block.shape[dim] - width, None, axis...  24.2 us
    ppermute x2, starting transfers between devices, passed_along(): return lax.ppermute(array, axis, pairs)  11 us
    unnamed x91, local copies, waits for them, and re-layouts  9.01 us
    ppermute x6, starting transfers between devices, padded_2(): lax.ppermute(lax.slice_in_dim(block, 0, width, axis=dim), axis, backward)  7.75 us
    dot_general x2, matrix products, forward_part(): jnp.dot(row_patches(ext, rows), flat_now, preferred_element_type=jnp.floa...  6.41 us
    dot_general x2, matrix products, backward_part(): lax.dot_general(patches, slope_grad, (((0,), (0,)), ((), ())), preferred_...  4.98 us
    convert_element_type x1, other arithmetic, update_part(): new_flat = (flat_now - 0.05 * new_moment).astype(jnp.bfloat16)  4.45 us
  transfers between devices with their start and end apart: 15, of which 4 were waited for; matrix products, arithmetic and copies ran while one was open for 16% of the time, Pallas kernels for 0%

commit v1 on v0

--- a/solution.py
+++ b/solution.py
@@ -3,6 +3,8 @@
 import jax
 import jax.numpy as jnp
 from jax import lax
+from jax.experimental import pallas as pl
+from jax.experimental.pallas import tpu as pltpu
 from jax.sharding import PartitionSpec as P
 
 C = 256
@@ -112,6 +114,447 @@
     return (out_acts[None], in_grad[None], w_now[None], w_old[None], moment.reshape(1, 3, 3, C, C))
 
 
+SWAP = [(0, 1), (1, 0)]
+BF16 = jnp.bfloat16
+F32 = jnp.float32
+NT = (((1,), (1,)), ((), ()))
+TN = (((0,), (0,)), ((), ()))
+MIB = 2**20
+
+
+def vmem(count):
+    return [pl.BlockSpec(memory_space=pltpu.VMEM)] * count
+
+
+def anywhere(count):
+    return [pl.BlockSpec(memory_space=pl.ANY)] * count
+
+
+SMEM = pl.BlockSpec(memory_space=pltpu.SMEM)
+
+
+def call(kernel, outs, in_specs, out_specs, scratch, macs, limit=24):
+    return pl.pallas_call(
+        kernel,
+        out_shape=[jax.ShapeDtypeStruct(shape, kind) for shape, kind in outs],
+        in_specs=in_specs,
+        out_specs=out_specs,
+        scratch_shapes=scratch,
+        compiler_params=pltpu.CompilerParams(vmem_limit_bytes=limit * MIB),
+        cost_estimate=pl.CostEstimate(
+            flops=2 * macs, bytes_accessed=MIB, transcendentals=0
+        ),
+    )
+
+
+def conv_rows(rows_of, start, count, taps):
+    lhs = [rows_of[pl.ds(start + ky, count)] for ky in range(3)]
+    wcol = lhs[0].shape[1]
+    lhs = jnp.concatenate([part.reshape(count * wcol, C) for part in lhs], axis=1)
+    left, mid, right = (
+        part.reshape(count, wcol, C) for part in (taps(lhs, 0), taps(lhs, 1), taps(lhs, 2))
+    )
+    col = lax.broadcasted_iota(jnp.int32, mid.shape, 1)
+    left = jnp.where(col == 0, 0.0, pltpu.roll(left, 1, 1))
+    right = jnp.where(col == wcol - 1, 0.0, pltpu.roll(right, wcol - 1, 1))
+    return (left + mid + right) * (1.0 / math.sqrt(9 * C))
+
+
+def taps_of(kernel_ref):
+    def taps(lhs, kx):
+        rhs = jnp.concatenate([kernel_ref[0, ky, kx] for ky in range(3)], axis=0)
+        return jnp.dot(lhs, rhs, preferred_element_type=F32)
+
+    return taps
+
+
+def flipped_taps_of(kernel_ref):
+    def taps(lhs, kx):
+        rhs = jnp.concatenate([kernel_ref[0, 2 - ky, 2 - kx] for ky in range(3)], axis=1)
+        return lax.dot_general(lhs, rhs, NT, preferred_element_type=F32)
+
+    return taps
+
+
+def chunks(count):
+    return [(at, min(2, count - at)) for at in range(0, count, 2)]
+
+
+def silu_rows(maps, kernel_ref, count, out_ref):
+    for at, size in chunks(count):
+        pre = conv_rows(maps, at, size, taps_of(kernel_ref))
+        out_ref[pl.ds(at, size)] = (pre / (1.0 + jnp.exp(-pre))).astype(BF16)
+
+
+def slope_rows(maps, start, kernel_ref, grads, count, dz3, to):
+    for at, size in chunks(count):
+        back = conv_rows(maps, start + at, size, taps_of(kernel_ref))
+        sig = 1.0 / (1.0 + jnp.exp(-back))
+        dz = grads[pl.ds(at, size)].astype(F32) * (sig * (1.0 + back * (1.0 - sig)))
+        wcol = dz.shape[1]
+        col = lax.broadcasted_iota(jnp.int32, dz.shape, 1)
+        row = pl.ds(to + at, size)
+        dz3[row, :, 0:C] = jnp.where(col == 0, 0.0, pltpu.roll(dz, 1, 1)).astype(BF16)
+        dz3[row, :, C : 2 * C] = dz.astype(BF16)
+        dz3[row, :, 2 * C :] = jnp.where(
+            col == wcol - 1, 0.0, pltpu.roll(dz, wcol - 1, 1)
+        ).astype(BF16)
+
+
+class Middle:
+    def __init__(self, dz3):
+        self.dz3 = dz3
+
+    def __getitem__(self, rows):
+        return self.dz3[rows, :, C : 2 * C]
+
+
+def in_grad_rows(dz3, kernel_ref, count, out_ref):
+    for at, size in chunks(count):
+        dx = conv_rows(Middle(dz3), at, size, flipped_taps_of(kernel_ref))
+        out_ref[pl.ds(at, size)] = dx.astype(BF16)
+
+
+def kernel_grad(maps, start, dz3, dz_start, rows, ky):
+    wcol = maps.shape[1]
+    lhs = maps[pl.ds(start + ky, rows)].reshape(rows * wcol, C)
+    rhs = dz3[pl.ds(dz_start, rows)].reshape(rows * wcol, 3 * C)
+    grad = lax.dot_general(lhs, rhs, TN, preferred_element_type=F32) * (1.0 / math.sqrt(9 * C))
+    return [grad[:, (2 - kx) * C : (3 - kx) * C] for kx in range(3)]
+
+
+def zero_row(ref, at):
+    ref[pl.ds(at, 1)] = jnp.zeros((1,) + ref.shape[1:], ref.dtype)
+
+
+def put(ref, at, value):
+    ref[pl.ds(at, value.shape[0])] = value
+
+
+def put_second_map(ref, at, slots, x_in, stash):
+    same = slots[0, 0] == slots[1, 0]
+
+    @pl.when(same)
+    def _():
+        put(ref, at, x_in[0])
+
+    @pl.when(jnp.logical_not(same))
+    def _():
+        put(ref, at, stash[0, slots[1, 0]])
+
+
+def edge(rows, count, me):
+    return pl.ds((1 - me) * (rows - count), count)
+
+
+def inner(rows, count, me):
+    return pl.ds(me * (rows - count), count)
+
+
+def run_copies(copies, sems):
+    started = [pltpu.make_async_copy(a, b, sems.at[i]) for i, (a, b) in enumerate(copies)]
+    for copy in started:
+        copy.start()
+    for copy in started:
+        copy.wait()
+
+
+def pack_first(slots, x_in, stash, grad, next_in, next_g, halo, edges, sems):
+    me = lax.axis_index("band")
+    pos = lax.axis_index("segment")
+    rows = x_in.shape[1]
+    turn = jnp.maximum(pos - (lax.axis_size("segment") - rows), 0)
+    run_copies(
+        [
+            (x_in.at[0, edge(rows, 2, me)], halo.at[pl.ds(0, 2)]),
+            (stash.at[0, slots[0, 0], edge(rows, 3, me)], edges.at[pl.ds(0, 3)]),
+            (grad.at[0, edge(rows, 2, me)], edges.at[pl.ds(3, 2)]),
+        ],
+        sems,
+    )
+
+    @pl.when(pos == 0)
+    def _():
+        run_copies([(next_in.at[edge(rows, 1, me)], halo.at[pl.ds(2, 1)])], sems)
+
+    @pl.when(pos != 0)
+    def _():
+        run_copies([(next_g.at[pl.ds(turn, 1)], halo.at[pl.ds(2, 1)])], sems)
+
+
+def pack_second(slots, x_in, stash, grad, rest, edges2, rest2, sems):
+    me = lax.axis_index("band")
+    rows = x_in.shape[1]
+    copies = [
+        (stash.at[0, slots[0, 0], inner(rows, rows - 3, me)], rest.at[pl.ds(0, rows - 3)]),
+        (grad.at[0, inner(rows, rows - 2, me)], rest.at[pl.ds(rows - 3, rows - 2)]),
+    ]
+    same = slots[0, 0] == slots[1, 0]
+
+    @pl.when(same)
+    def _():
+        run_copies(
+            copies
+            + [
+                (x_in.at[0, edge(rows, 2, me)], edges2),
+                (x_in.at[0, inner(rows, rows - 2, me)], rest2),
+            ],
+            sems,
+        )
+
+    @pl.when(jnp.logical_not(same))
+    def _():
+        run_copies(
+            copies
+            + [
+                (stash.at[0, slots[1, 0], edge(rows, 2, me)], edges2),
+                (stash.at[0, slots[1, 0], inner(rows, rows - 2, me)], rest2),
+            ],
+            sems,
+        )
+
+
+def forward_one(x_in, halo, w_now, y1, maps):
+    me = lax.axis_index("band")
+    rows = x_in.shape[1]
+    zero_row(maps, (rows + 2) * me)
+    put(maps, 1 + me, x_in[0])
+    put(maps, (rows + 1) * (1 - me), halo[0:2])
+    silu_rows(maps, w_now, rows + 1, y1)
+
+
+def forward_two(next_in, halo, arrived, w_one, act, maps):
+    me = lax.axis_index("band")
+    first = lax.axis_index("segment") == 0
+    rows = next_in.shape[0]
+    zero_row(maps, (rows + 1) * me)
+
+    @pl.when(first)
+    def _():
+        put(maps, 1, next_in[...])
+        put(maps, (rows + 1) * (1 - me), halo[2:3])
+
+    @pl.when(jnp.logical_not(first))
+    def _():
+        put(maps, 1 - me, arrived[...])
+
+    silu_rows(maps, w_one, rows, act.at[0])
+
+
+def backward_one(slots, stash, grad, edges, w_old, dx, own_kgrad, dz3_edge, maps, grads, dz3):
+    me = lax.axis_index("band")
+    rows = stash.shape[2]
+    zero_row(maps, (rows + 3) * me)
+    put(maps, 1 + 2 * me, stash[0, slots[0, 0]])
+    put(maps, (rows + 1) * (1 - me), edges[0:3])
+    put(grads, 2 * me, grad[0])
+    put(grads, rows * (1 - me), edges[3:5])
+    zero_row(dz3, (rows + 2) * me)
+    slope_rows(maps, 0, w_old, grads, rows + 2, dz3, 1 - me)
+    in_grad_rows(dz3, w_old, rows + 1, dx)
+    dz3_edge[...] = dz3[pl.ds((rows + 1) * (1 - me), 2)]
+    for ky in range(3):
+        taps = kernel_grad(maps, 2 * me, dz3, 1 + me, rows, ky)
+        for kx in range(3):
+            own_kgrad[ky, kx] = taps[kx]
+
+
+def backward_one_rest(slots, stash, edges, rest, dz3_edge, w_old, dx, maps, dz3):
+    me = lax.axis_index("band")
+    rows = stash.shape[2]
+    zero_row(maps, (rows + 1) * (1 - me))
+    put(maps, (rows + 1) * me, stash[0, slots[0, 0], edge(rows, 1, me)])
+    put(maps, 1 + (rows - 3) * me, edges[0:3])
+    put(maps, 4 - 3 * me, rest[0 : rows - 3])
+    zero_row(dz3, rows * (1 - me))
+    put(dz3, (rows - 1) * me, dz3_edge[...])
+    slope_rows(
+        maps, 2 * (1 - me), w_old, rest.at[pl.ds(rows - 3, rows - 2)], rows - 2, dz3, 2 - me
+    )
+    in_grad_rows(dz3, w_old, rows - 1, dx)
+
+
+def update_one(maps, dz3, own_kgrad, moment, w_now, m_one, w_one):
+    me = lax.axis_index("band")
+    rows = maps.shape[0] - 2
+    for ky in range(3):
+        taps = kernel_grad(maps, 0, dz3, me, rows, ky)
+        for kx in range(3):
+            fresh = 0.9 * moment[0, ky, kx] + (own_kgrad[ky, kx] + taps[kx])
+            m_one[ky, kx] = fresh
+            w_one[0, ky, kx] = (w_now[0, ky, kx].astype(F32) - 0.05 * fresh).astype(BF16)
+
+
+def backward_two(
+    slots, x_in, stash, edges2, returned, next_g, next_g_other, w_now,
+    dx, own_kgrad, dz3_edge, maps, grads, dz3,
+):
+    me = lax.axis_index("band")
+    last = lax.axis_index("segment") == lax.axis_size("segment") - 1
+    rows = stash.shape[2]
+    zero_row(maps, (rows + 2) * me)
+    put_second_map(maps, 1 + me, slots, x_in, stash)
+    put(maps, (rows + 1) * (1 - me), edges2[...])
+
+    @pl.when(last)
+    def _():
+        put(grads, me, next_g[...])
+        put(grads, rows * (1 - me), next_g_other[pl.ds((rows - 1) * me, 1)])
+
+    @pl.when(jnp.logical_not(last))
+    def _():
+        put(grads, 0, returned[...])
+
+    zero_row(dz3, (rows + 1) * me)
+    slope_rows(maps, 0, w_now, grads, rows + 1, dz3, 1 - me)
+    in_grad_rows(dz3, w_now, rows, dx.at[0])
+    dz3_edge[...] = dz3[pl.ds((rows + 1) * (1 - me), 1)]
+    for ky in range(3):
+        taps = kernel_grad(maps, me, dz3, 1, rows, ky)
+        for kx in range(3):
+            own_kgrad[ky, kx] = taps[kx]
+
+
+def backward_two_rest(
+    slots, x_in, stash, edges2, rest2, dz3_edge, returned, next_g_other, w_now,
+    own_kgrad, m_one, w_one, m_out, w_out, maps, own, grads, dz3, m_two, w_two, sems,
+):
+    me = lax.axis_index("band")
+    last = lax.axis_index("segment") == lax.axis_size("segment") - 1
+    rows = stash.shape[2]
+    zero_row(maps, (rows + 1) * (1 - me))
+    put_second_map(own, 0, slots, x_in, stash)
+    put(maps, (rows + 1) * me, own[edge(rows, 1, me)])
+    put(maps, 1 + (rows - 2) * me, edges2[...])
+    put(maps, 3 - 2 * me, rest2[...])
+
+    @pl.when(last)
+    def _():
+        put(grads, 0, next_g_other[pl.ds(1 - me, rows - 1)])
+
+    @pl.when(jnp.logical_not(last))
+    def _():
+        put(grads, 0, returned[...])
+
+    put(dz3, (rows - 1) * me, dz3_edge[...])
+    slope_rows(maps, 1 - me, w_now, grads, rows - 1, dz3, 1 - me)
+    copies = []
+    for ky in range(3):
+        taps = kernel_grad(maps, 0, dz3, 0, rows, ky)
+        for kx in range(3):
+            fresh = 0.9 * m_one[ky, kx] + (own_kgrad[ky, kx] + taps[kx])
+            m_two[ky, kx] = fresh
+            w_two[ky, kx] = (w_one[0, ky, kx].astype(F32) - 0.05 * fresh).astype(BF16)
+        for at, (source, target) in enumerate(((m_two, m_out), (w_two, w_out))):
+            copy = pltpu.make_async_copy(source.at[ky], target.at[0, ky], sems.at[2 * ky + at])
+            copy.start()
+            copies.append(copy)
+    for copy in copies:
+        copy.wait()
+
+
+def gathered_at_last(row, rows):
+    first = lax.axis_size("segment") - rows
+    width = 1
+    while width < rows:
+        pairs = [
+            (first + at + width - 1, first + at + 2 * width - 1)
+            for at in range(0, rows, 2 * width)
+        ]
+        row = jnp.concatenate([lax.ppermute(row, "segment", pairs), row], axis=0)
+        width *= 2
+    return row
+
+
+def two_band_body(
+    first_input, stashed, first_grad, weight_now, weight_old, momentum, slot_plan,
+    next_input, next_grad,
+):
+    rows, wcol = first_input.shape[1:3]
+    unit = rows * wcol * 9 * C * C
+    full = (3, 3, C, C)
+
+    def some(count):
+        return ((count, wcol, C), BF16)
+
+    def map_rows(count):
+        return pltpu.VMEM((count, wcol, C), BF16)
+
+    def dz_rows(count):
+        return pltpu.VMEM((count, wcol, 3 * C), BF16)
+
+    def swapped(array):
+        return lax.ppermute(array, "band", SWAP)
+
+    halo, edges = call(
+        pack_first, [some(3), some(5)], [SMEM] + anywhere(5), anywhere(2),
+        [pltpu.SemaphoreType.DMA((3,))], 0,
+    )(slot_plan, first_input, stashed, first_grad, next_input, next_grad)
+    halo = swapped(halo)
+    edges = swapped(edges)
+    rest, edges2, rest2 = call(
+        pack_second, [some(2 * rows - 5), some(2), some(rows - 2)], [SMEM] + anywhere(3),
+        anywhere(3), [pltpu.SemaphoreType.DMA((4,))], 0,
+    )(slot_plan, first_input, stashed, first_grad)
+    rest = swapped(rest)
+    edges2 = swapped(edges2)
+    rest2 = swapped(rest2)
+    next_grad_other = gathered_at_last(halo[2:3], rows)
+
+    (y1,) = call(
+        forward_one, [some(rows + 1)], vmem(3), vmem(1), [map_rows(rows + 3)], unit
+    )(first_input, halo, weight_now)
+    arrived = passed_along(y1, "segment", 1)
+
+    dx_a, own_kgrad, dz3_edge = call(
+        backward_one, [some(rows + 1), (full, F32), ((2, wcol, 3 * C), BF16)],
+        [SMEM] + vmem(4), vmem(3),
+        [map_rows(rows + 4), map_rows(rows + 2), dz_rows(rows + 3)], 3 * unit,
+    )(slot_plan, stashed, first_grad, edges, weight_old)
+    returned_a = passed_along(dx_a, "segment", -1)
+
+    dx_b, maps, dz3 = call(
+        backward_one_rest,
+        [some(rows - 1), some(rows + 2), ((rows + 1, wcol, 3 * C), BF16)],
+        [SMEM] + vmem(5), vmem(3), [], 2 * unit,
+    )(slot_plan, stashed, edges, rest, dz3_edge, weight_old)
+    returned_b = passed_along(dx_b, "segment", -1)
+
+    m_one, w_one = call(
+        update_one, [(full, F32), ((1,) + full, BF16)], vmem(5), vmem(2), [], unit
+    )(maps, dz3, own_kgrad, momentum, weight_now)
+
+    dx, own_kgrad, dz3_edge = call(
+        backward_two,
+        [((1, rows, wcol, C), BF16), (full, F32), ((1, wcol, 3 * C), BF16)],
+        [SMEM] + vmem(7), vmem(3),
+        [map_rows(rows + 3), map_rows(rows + 1), dz_rows(rows + 2)], 3 * unit,
+    )(slot_plan, first_input, stashed, edges2, returned_a, next_grad, next_grad_other, weight_now)
+
+    (act,) = call(
+        forward_two, [((1, rows, wcol, C), BF16)], vmem(4), vmem(1), [map_rows(rows + 2)], unit
+    )(next_input, halo, arrived, w_one)
+
+    m_two, w_two = call(
+        backward_two_rest,
+        [((1,) + full, F32), ((1,) + full, BF16)],
+        [SMEM] + vmem(11), anywhere(2),
+        [
+            map_rows(rows + 2), map_rows(rows), map_rows(rows - 1), dz_rows(rows),
+            pltpu.VMEM(full, F32), pltpu.VMEM(full, BF16), pltpu.SemaphoreType.DMA((6,)),
+        ],
+        2 * unit,
+    )(
+        slot_plan, first_input, stashed, edges2, rest2, dz3_edge, returned_b, next_grad_other,
+        weight_now, own_kgrad, m_one, w_one,
+    )
+    return act, dx, w_two, w_one, m_two
+
+
+def fits_two_bands(mesh):
+    return mesh.shape["band"] == 2 and mesh.shape["segment"] >= 8
+
+
 def solution(mesh):
     placed = (
         P("segment", "band", None, None),
@@ -125,7 +568,7 @@
         P("band", None, None),
     )
     return jax.shard_map(
-        body,
+        two_band_body if fits_two_bands(mesh) else body,
         mesh=mesh,
         in_specs=placed,
         out_specs=(

time: 188 us -> 65.6 us (0.35); the launches traced: 185 us -> 65.1 us
  waiting for transfers between devices: 73.6 us -> 6.4 us
  Pallas kernels: 0 us -> 28.6 us
  starting transfers between devices: 43 us -> 21.5 us
  matrix products: 18.2 us -> 0 us
  between operations: 19 us -> 1.04 us
  other arithmetic: 12.2 us -> 0.13 us
  local copies, waits for them, and re-layouts: 19.4 us -> 7.45 us
    psum x1 -> x0, waiting for transfers between devices: 67.3 us -> none  [update_part(): total = lax.psum(kgrad.astype(jnp.bfloat16), 'band').astype(jnp.float32)]
    pallas_call x0 -> x9, Pallas kernels: none -> 28.6 us  [the longest x1 5.72 us: two_band_body(): call(backward_one, [some(rows + 1), (full, F32), ((2, wcol, 3 * C), BF16)...]
    ppermute x12 -> x8, starting transfers between devices: 31.9 us -> 10 us  [the longest x5 6.15 us: swapped(): return lax.ppermute(array, 'band', SWAP)]
    dot_general x8 -> x0, matrix products: 18.2 us -> none  [the longest x2 6.41 us: forward_part(): jnp.dot(row_patches(ext, rows), flat_now, preferred_element_type=jnp.floa...]
    slice x12 -> x1, local copies, waits for them, and re-layouts: 5.24 us -> 0.01 us  [two_band_body(): next_grad_other = gathered_at_last(halo[2:3], rows)]
    convert_element_type x1 -> x0, other arithmetic: 4.45 us -> none  [update_part(): new_flat = (flat_now - 0.05 * new_moment).astype(jnp.bfloat16)]
    concatenate x11 -> x3, other arithmetic: 4.19 us -> 0.13 us  [gathered_at_last(): row = jnp.concatenate([lax.ppermute(row, 'segment', pairs), row], axis=0)]
    ppermute x12 -> x8, waiting for transfers between devices: 2.74 us -> 6.39 us  [the longest x5 5.42 us: swapped(): return lax.ppermute(array, 'band', SWAP)]
  transfers between devices with their start and end apart: 15 -> 11, of which waited for: 4 -> 3; matrix products, arithmetic and copies ran while one was open for 16% -> 0% of each run, Pallas kernels for 0% -> 34%
where the time goes in v1:
time: 65.6 us; the launch traced here: 65.1 us
  Pallas kernels  28.6 us (44%)
  starting transfers between devices  21.5 us (33%)
  local copies, waits for them, and re-layouts  7.45 us (11%)
  waiting for transfers between devices  6.4 us (10%)
  between operations  1.04 us (2%)
    ppermute x3, starting transfers between devices, passed_along(): return lax.ppermute(array, axis, pairs)  11.5 us
    unnamed x31, local copies, waits for them, and re-layouts  7.45 us
    ppermute x5, starting transfers between devices, swapped(): return lax.ppermute(array, 'band', SWAP)  6.15 us
    pallas_call x1, Pallas kernels, two_band_body(): call(backward_one, [some(rows + 1), (full, F32), ((2, wcol, 3 * C), BF16)...  5.72 us
    ppermute x5, waiting for transfers between devices, swapped(): return lax.ppermute(array, 'band', SWAP)  5.42 us
    pallas_call x1, Pallas kernels, two_band_body(): call(backward_two, [((1, rows, wcol, C), BF16), (full, F32), ((1, wcol, 3...  5.07 us
    pallas_call x1, Pallas kernels, two_band_body(): call(backward_two_rest, [((1,) + full, F32), ((1,) + full, BF16)], [SMEM]...  5.02 us
    ppermute x3, starting transfers between devices, gathered_at_last(): row = jnp.concatenate([lax.ppermute(row, 'segment', pairs), row], axis=0)  3.86 us
  transfers between devices with their start and end apart: 11, of which 3 were waited for; matrix products, arithmetic and copies ran while one was open for 0% of the time, Pallas kernels for 34%

profile of v1, /device:TPU:27, one launch (start us, length us, event | category | flops | bytes accessed | tf_op | source)
XLA Modules:
  0.0 65.1 jit_solution(6898303558274660498)
XLA Ops:
  1.4 1.2 %copy-done = bf16[1,2,8,128,256]{4,3,2,1,0:T(8,128)(2,1)S(1)} copy-done((bf16[1,2,8,128,256]{4,3,2,1,0:T(8,128)(2,1)S(1)}, bf16[1,2,8,128,256]{4,3,2,1,0:T(8,128)(2,1)}, u32[]{:S(2)}) %copy-start) | copy-done | bytes 1048600
  4.7 1.0 %copy-done.10 = bf16[8,128,256]{2,1,0:T(8,128)(2,1)S(1)} copy-done((bf16[8,128,256]{2,1,0:T(8,128)(2,1)S(1)}, bf16[8,128,256]{2,1,0:T(8,128)(2,1)}, u32[]{:S(2)}) %copy-start.10) | copy-done | bytes 524312
  5.7 1.0 %copy-done.12 = bf16[8,128,256]{2,1,0:T(8,128)(2,1)S(1)} copy-done((bf16[8,128,256]{2,1,0:T(8,128)(2,1)S(1)}, bf16[8,128,256]{2,1,0:T(8,128)(2,1)}, u32[]{:S(2)}) %copy-start.12) | copy-done | bytes 524312
  6.8 1.3 %shard_map.128 = (bf16[3,128,256]{2,1,0:T(8,128)(2,1)S(1)}, bf16[5,128,256]{2,1,0:T(8,128)(2,1)S(1)}) custom-call(s32[2,1]{1,0:T(2,128)S(1)} %copy.14.slots, bf16[1,8,128,256]{3,2,1,0:T(8,128)(2,1)S(1)} %copy-done.3, bf16[1,2,8,128,256]{4,3,2,1,0:T(8,128)(2,1)S(1)} %copy-done, bf16[1,8,128,256]{3,2,1,0:T(8,128)(2,1)S(1)} %copy-done.6, ...), custom_call_target="tpu_custom_call" | custom-call | bytes 1048576 | tf_op jit(solution)/shard_map/pallas_call | solution.py:489
  8.1 1.3 %collective-permute-start = (bf16[3,128,256]{2,1,0:T(8,128)(2,1)S(1)}, bf16[3,128,256]{2,1,0:T(8,128)(2,1)S(1)}, u32[]{:S(2)}, u32[]{:S(2)}) collective-permute-start(bf16[3,128,256]{2,1,0:T(8,128)(2,1)S(1)} %get-tuple-element.23), channel_id=1, source_target_pairs={{0,1},{1,0},{2,3},{3,2},{4,5},{5,4},{6,7},{7,6},{8,9},{9,8},{10,11... | collective-permute-start | bytes 589832 | tf_op jit(solution)/shard_map/ppermute | solution.py:487
  9.4 4.5 %collective-permute-done.halo = bf16[3,128,256]{2,1,0:T(8,128)(2,1)S(1)} collective-permute-done((bf16[3,128,256]{2,1,0:T(8,128)(2,1)S(1)}, bf16[3,128,256]{2,1,0:T(8,128)(2,1)S(1)}, u32[]{:S(2)}, u32[]{:S(2)}) %collective-permute-start) | collective-permute-done | bytes 196640 | tf_op jit(solution)/shard_map/ppermute | solution.py:487
  13.9 1.3 %collective-permute-start.6 = (bf16[1,128,256]{2,1,0:T(8,128)(2,1)S(1)}, bf16[1,128,256]{2,1,0:T(8,128)(2,1)S(1)}, u32[]{:S(2)}, u32[]{:S(2)}) collective-permute-start(bf16[1,128,256]{2,1,0:T(8,128)(2,1)S(1)} %slice.4), channel_id=1, source_target_pairs={{16,18},{20,22},{24,26},{28,30},{17,19},{21,23},{25,27},{29,31}} | collective-permute-start | bytes 196616 | tf_op jit(solution)/shard_map/ppermute | solution.py:464
  15.2 1.3 %collective-permute-start.2 = (bf16[5,128,256]{2,1,0:T(8,128)(2,1)S(1)}, bf16[5,128,256]{2,1,0:T(8,128)(2,1)S(1)}, u32[]{:S(2)}, u32[]{:S(2)}) collective-permute-start(bf16[5,128,256]{2,1,0:T(8,128)(2,1)S(1)} %get-tuple-element.24), channel_id=1, source_target_pairs={{0,1},{1,0},{2,3},{3,2},{4,5},{5,4},{6,7},{7,6},{8,9},{9,8},{10,11... | collective-permute-start | bytes 983048 | tf_op jit(solution)/shard_map/ppermute | solution.py:487
  17.5 1.3 %collective-permute-start.7 = (bf16[2,128,256]{2,1,0:T(8,128)(2,1)S(1)}, bf16[2,128,256]{2,1,0:T(8,128)(2,1)S(1)}, u32[]{:S(2)}, u32[]{:S(2)}) collective-permute-start(bf16[2,128,256]{2,1,0:T(8,128)(2,1)S(1)} %pad_maximum_fusion.2), channel_id=1, source_target_pairs={{18,22},{26,30},{19,23},{27,31}} | collective-permute-start | bytes 393224 | tf_op jit(solution)/shard_map/ppermute | solution.py:464
  18.8 1.2 %shard_map.130 = (bf16[11,128,256]{2,1,0:T(8,128)(2,1)S(1)}, bf16[2,128,256]{2,1,0:T(8,128)(2,1)S(1)}, bf16[6,128,256]{2,1,0:T(8,128)(2,1)S(1)}) custom-call(s32[2,1]{1,0:T(2,128)S(1)} %copy.14.slots, bf16[1,8,128,256]{3,2,1,0:T(8,128)(2,1)S(1)} %copy-done.3, bf16[1,2,8,128,256]{4,3,2,1,0:T(8,128)(2,1)S(1)} %copy-done, bf16[1,8,128,256]{3,2,1,0:T(8,128)(2,1)S(1)} %copy-done.6), custom_call_target="tpu_custom_call" | custom-call | bytes 1048576 | tf_op jit(solution)/shard_map/pallas_call | solution.py:495
  20.1 1.3 %collective-permute-start.3 = (bf16[11,128,256]{2,1,0:T(8,128)(2,1)S(1)}, bf16[11,128,256]{2,1,0:T(8,128)(2,1)S(1)}, u32[]{:S(2)}, u32[]{:S(2)}) collective-permute-start(bf16[11,128,256]{2,1,0:T(8,128)(2,1)S(1)} %get-tuple-element.25), channel_id=1, source_target_pairs={{0,1},{1,0},{2,3},{3,2},{4,5},{5,4},{6,7},{7,6},{8,9},{9,8},{10,11... | collective-permute-start | bytes 2162696 | tf_op jit(solution)/shard_map/ppermute | solution.py:487
  21.4 1.7 %shard_map.129 = bf16[9,128,256]{2,1,0:T(8,128)(2,1)S(1)} custom-call(bf16[1,8,128,256]{3,2,1,0:T(8,128)(2,1)S(1)} %copy-done.4, bf16[3,128,256]{2,1,0:T(8,128)(2,1)S(1)} %collective-permute-done.halo, bf16[1,3,3,256,256]{4,3,2,1,0:T(8,128)(2,1)S(1)} %copy-done.2), custom_call_target="tpu_custom_call" | custom-call | flops 1207959552 | bytes 1048576 | tf_op jit(solution)/shard_map/pallas_call | solution.py:504
  23.0 1.3 %collective-permute-start.1 = (bf16[9,128,256]{2,1,0:T(8,128)(2,1)S(1)}, bf16[9,128,256]{2,1,0:T(8,128)(2,1)S(1)}, u32[]{:S(2)}, u32[]{:S(2)}) collective-permute-start(bf16[9,128,256]{2,1,0:T(8,128)(2,1)S(1)} %shard_map.129), channel_id=1, source_target_pairs={{0,2},{2,4},{4,6},{6,8},{8,10},{10,12},{12,14},{14,16},{16,18},{18... | collective-permute-start | bytes 1769480 | tf_op jit(solution)/shard_map/ppermute | solution.py:29
  24.4 1.3 %collective-permute-start.8 = (bf16[4,128,256]{2,1,0:T(8,128)(2,1)S(1)}, bf16[4,128,256]{2,1,0:T(8,128)(2,1)S(1)}, u32[]{:S(2)}, u32[]{:S(2)}) collective-permute-start(bf16[4,128,256]{2,1,0:T(8,128)(2,1)S(1)} %pad_maximum_fusion.1), channel_id=1, source_target_pairs={{22,30},{23,31}} | collective-permute-start | bytes 786440 | tf_op jit(solution)/shard_map/ppermute | solution.py:464
  25.7 5.7 %shard_map.131 = (bf16[9,128,256]{2,1,0:T(8,128)(2,1)S(1)}, f32[3,3,256,256]{3,2,1,0:T(8,128)S(1)}, bf16[2,128,768]{2,1,0:T(8,128)(2,1)S(1)}) custom-call(s32[2,1]{1,0:T(2,128)S(1)} %copy.14.slots, bf16[1,2,8,128,256]{4,3,2,1,0:T(8,128)(2,1)S(1)} %copy-done.1, bf16[1,8,128,256]{3,2,1,0:T(8,128)(2,1)S(1)} %copy-done.7, ...), custom_call_target="tpu_custom_call" | custom-call | flops 3623878656 | bytes 1048576 | tf_op jit(solution)/shard_map/pallas_call | solution.py:509
  31.5 3.7 %collective-permute-start.5 = (bf16[9,128,256]{2,1,0:T(8,128)(2,1)S(1)}, bf16[9,128,256]{2,1,0:T(8,128)(2,1)S(1)}, u32[]{:S(2)}, u32[]{:S(2)}) collective-permute-start(bf16[9,128,256]{2,1,0:T(8,128)(2,1)S(1)} %get-tuple-element.32), channel_id=1, source_target_pairs={{2,0},{4,2},{6,4},{8,6},{10,8},{12,10},{14,12},{16,14},{18,16},{20... | collective-permute-start | bytes 1769480 | tf_op jit(solution)/shard_map/ppermute | solution.py:29
  35.1 1.3 %collective-permute-start.4 = (bf16[2,128,256]{2,1,0:T(8,128)(2,1)S(1)}, bf16[2,128,256]{2,1,0:T(8,128)(2,1)S(1)}, u32[]{:S(2)}, u32[]{:S(2)}) collective-permute-start(bf16[2,128,256]{2,1,0:T(8,128)(2,1)S(1)} %get-tuple-element.31), channel_id=1, source_target_pairs={{0,1},{1,0},{2,3},{3,2},{4,5},{5,4},{6,7},{7,6},{8,9},{9,8},{10,11... | collective-permute-start | bytes 393224 | tf_op jit(solution)/shard_map/ppermute | solution.py:487
  38.4 3.3 %shard_map.132 = (bf16[7,128,256]{2,1,0:T(8,128)(2,1)S(1)}, bf16[10,128,256]{2,1,0:T(8,128)(2,1)S(1)}, bf16[9,128,768]{2,1,0:T(8,128)(2,1)S(1)}) custom-call(s32[2,1]{1,0:T(2,128)S(1)} %copy.14.slots, bf16[1,2,8,128,256]{4,3,2,1,0:T(8,128)(2,1)S(1)} %copy-done.1, bf16[5,128,256]{2,1,0:T(8,128)(2,1)S(1)} %collective-permute-done.2.edges, ...), custom_call_target="tpu_custom_call" | custom-call | flops 2415919104 | bytes 1048576 | tf_op jit(solution)/shard_map/pallas_call | solution.py:516
  41.6 6.5 %collective-permute-start.10 = (bf16[7,128,256]{2,1,0:T(8,128)(2,1)S(1)}, bf16[7,128,256]{2,1,0:T(8,128)(2,1)S(1)}, u32[]{:S(2)}, u32[]{:S(2)}) collective-permute-start(bf16[7,128,256]{2,1,0:T(8,128)(2,1)S(1)} %get-tuple-element.36), channel_id=1, source_target_pairs={{2,0},{4,2},{6,4},{8,6},{10,8},{12,10},{14,12},{16,14},{18,16},{20... | collective-permute-start | bytes 1376264 | tf_op jit(solution)/shard_map/ppermute | solution.py:29
  48.2 2.8 %shard_map.133 = (f32[3,3,256,256]{3,2,1,0:T(8,128)S(1)}, bf16[1,3,3,256,256]{4,3,2,1,0:T(8,128)(2,1)}) custom-call(bf16[10,128,256]{2,1,0:T(8,128)(2,1)S(1)} %get-tuple-element.27.maps, bf16[9,128,768]{2,1,0:T(8,128)(2,1)S(1)} %get-tuple-element.28.dz3, f32[3,3,256,256]{3,2,1,0:T(8,128)S(1)} %get-tuple-element.29.own_kgrad, ...), custom_call_target="tpu_custom_call" | custom-call | flops 1207959552 | bytes 1048576 | tf_op jit(solution)/shard_map/pallas_call | solution.py:523
  51.0 1.3 %copy-done.8 = bf16[1,3,3,256,256]{4,3,2,1,0:T(8,128)(2,1)S(1)} copy-done((bf16[1,3,3,256,256]{4,3,2,1,0:T(8,128)(2,1)S(1)}, bf16[1,3,3,256,256]{4,3,2,1,0:T(8,128)(2,1)}, u32[]{:S(2)}) %copy-start.8) | copy-done | bytes 1179672
  52.2 2.5 %shard_map.134 = bf16[1,8,128,256]{3,2,1,0:T(8,128)(2,1)} custom-call(bf16[8,128,256]{2,1,0:T(8,128)(2,1)S(1)} %copy-done.11, bf16[3,128,256]{2,1,0:T(8,128)(2,1)S(1)} %collective-permute-done.halo, bf16[9,128,256]{2,1,0:T(8,128)(2,1)S(1)} %collective-permute-done.1.arrived, bf16[1,3,3,256,256]{4,3,2,1,0:T(8,128)(2,1)S(1)} %copy-done.8), custom_call_target="tpu_custom_call" | custom-call | flops 1207959552 | bytes 1048576 | tf_op jit(solution)/shard_map/pallas_call | solution.py:534
  54.8 5.1 %shard_map.135 = (bf16[1,8,128,256]{3,2,1,0:T(8,128)(2,1)}, f32[3,3,256,256]{3,2,1,0:T(8,128)S(1)}, bf16[1,128,768]{2,1,0:T(8,128)(2,1)S(1)}) custom-call(s32[2,1]{1,0:T(2,128)S(1)} %copy.14.slots, bf16[1,8,128,256]{3,2,1,0:T(8,128)(2,1)S(1)} %copy-done.4, bf16[1,2,8,128,256]{4,3,2,1,0:T(8,128)(2,1)S(1)} %copy-done.1, ...), custom_call_target="tpu_custom_call" | custom-call | flops 3623878656 | bytes 1048576 | tf_op jit(solution)/shard_map/pallas_call | solution.py:527
  59.9 5.0 %shard_map.136 = (f32[1,3,3,256,256]{4,3,2,1,0:T(8,128)}, bf16[1,3,3,256,256]{4,3,2,1,0:T(8,128)(2,1)}) custom-call(s32[2,1]{1,0:T(2,128)S(1)} %copy.14.slots, bf16[1,8,128,256]{3,2,1,0:T(8,128)(2,1)S(1)} %copy-done.4, bf16[1,2,8,128,256]{4,3,2,1,0:T(8,128)(2,1)S(1)} %copy-done.1, bf16[2,128,256]{2,1,0:T(8,128)(2,1)S(1)} %collective-permute-done.4.edges2, ...), custom_call_target="tpu_custom_call" | custom-call | flops 2415919104 | bytes 1048576 | tf_op jit(solution)/shard_map/pallas_call | solution.py:538
  (42 shorter events, 5.8 us)
Async XLA Ops:
  1.4 1.2 %copy-start = (bf16[1,2,8,128,256]{4,3,2,1,0:T(8,128)(2,1)S(1)}, bf16[1,2,8,128,256]{4,3,2,1,0:T(8,128)(2,1)}, u32[]{:S(2)}) copy-start(bf16[1,2,8,128,256]{4,3,2,1,0:T(8,128)(2,1)} %stash.11) | copy-start | bytes 3145732
  2.6 1.0 %copy-start.3 = (bf16[1,8,128,256]{3,2,1,0:T(8,128)(2,1)S(1)}, bf16[1,8,128,256]{3,2,1,0:T(8,128)(2,1)}, u32[]{:S(2)}) copy-start(bf16[1,8,128,256]{3,2,1,0:T(8,128)(2,1)} %x_in.9) | copy-start | bytes 1572868
  4.7 1.0 %copy-start.10 = (bf16[8,128,256]{2,1,0:T(8,128)(2,1)S(1)}, bf16[8,128,256]{2,1,0:T(8,128)(2,1)}, u32[]{:S(2)}) copy-start(bf16[8,128,256]{2,1,0:T(8,128)(2,1)} %next_in.3) | copy-start | bytes 1572868
  6.8 14.6 %copy-start.2 = (bf16[1,3,3,256,256]{4,3,2,1,0:T(8,128)(2,1)S(1)}, bf16[1,3,3,256,256]{4,3,2,1,0:T(8,128)(2,1)}, u32[]{:S(2)}) copy-start(bf16[1,3,3,256,256]{4,3,2,1,0:T(8,128)(2,1)} %w_now.7) | copy-start | bytes 3538948
  6.8 14.6 %copy-start.4 = (bf16[1,8,128,256]{3,2,1,0:T(8,128)(2,1)S(1)}, bf16[1,8,128,256]{3,2,1,0:T(8,128)(2,1)}, u32[]{:S(2)}) copy-start(bf16[1,8,128,256]{3,2,1,0:T(8,128)(2,1)} %x_in.9) | copy-start | bytes 1572868
  8.1 5.8 %collective-permute-start = (bf16[3,128,256]{2,1,0:T(8,128)(2,1)S(1)}, bf16[3,128,256]{2,1,0:T(8,128)(2,1)S(1)}, u32[]{:S(2)}, u32[]{:S(2)}) collective-permute-start(bf16[3,128,256]{2,1,0:T(8,128)(2,1)S(1)} %get-tuple-element.23), channel_id=1, source_target_pairs={{0,1},{1,0},{2,3},{3,2},{4,5},{5,4},{6,7},{7,6},{8,9},{9,8},{10,11... | collective-permute-start | bytes 589832 | tf_op jit(solution)/shard_map/ppermute | solution.py:487
  13.9 3.6 %collective-permute-start.6 = (bf16[1,128,256]{2,1,0:T(8,128)(2,1)S(1)}, bf16[1,128,256]{2,1,0:T(8,128)(2,1)S(1)}, u32[]{:S(2)}, u32[]{:S(2)}) collective-permute-start(bf16[1,128,256]{2,1,0:T(8,128)(2,1)S(1)} %slice.4), channel_id=1, source_target_pairs={{16,18},{20,22},{24,26},{28,30},{17,19},{21,23},{25,27},{29,31}} | collective-permute-start | bytes 196616 | tf_op jit(solution)/shard_map/ppermute | solution.py:464
  15.2 10.5 %collective-permute-start.2 = (bf16[5,128,256]{2,1,0:T(8,128)(2,1)S(1)}, bf16[5,128,256]{2,1,0:T(8,128)(2,1)S(1)}, u32[]{:S(2)}, u32[]{:S(2)}) collective-permute-start(bf16[5,128,256]{2,1,0:T(8,128)(2,1)S(1)} %get-tuple-element.24), channel_id=1, source_target_pairs={{0,1},{1,0},{2,3},{3,2},{4,5},{5,4},{6,7},{7,6},{8,9},{9,8},{10,11... | collective-permute-start | bytes 983048 | tf_op jit(solution)/shard_map/ppermute | solution.py:487
  17.5 6.9 %collective-permute-start.7 = (bf16[2,128,256]{2,1,0:T(8,128)(2,1)S(1)}, bf16[2,128,256]{2,1,0:T(8,128)(2,1)S(1)}, u32[]{:S(2)}, u32[]{:S(2)}) collective-permute-start(bf16[2,128,256]{2,1,0:T(8,128)(2,1)S(1)} %pad_maximum_fusion.2), channel_id=1, source_target_pairs={{18,22},{26,30},{19,23},{27,31}} | collective-permute-start | bytes 393224 | tf_op jit(solution)/shard_map/ppermute | solution.py:464
  20.0 5.7 %copy-start.1 = (bf16[1,2,8,128,256]{4,3,2,1,0:T(8,128)(2,1)S(1)}, bf16[1,2,8,128,256]{4,3,2,1,0:T(8,128)(2,1)}, u32[]{:S(2)}) copy-start(bf16[1,2,8,128,256]{4,3,2,1,0:T(8,128)(2,1)} %stash.11) | copy-start | bytes 3145732
  20.0 5.7 %copy-start.7 = (bf16[1,8,128,256]{3,2,1,0:T(8,128)(2,1)S(1)}, bf16[1,8,128,256]{3,2,1,0:T(8,128)(2,1)}, u32[]{:S(2)}) copy-start(bf16[1,8,128,256]{3,2,1,0:T(8,128)(2,1)} %grad.5) | copy-start | bytes 1572868
  20.1 5.7 %copy-start.14 = (bf16[1,3,3,256,256]{4,3,2,1,0:T(8,128)(2,1)S(1)}, bf16[1,3,3,256,256]{4,3,2,1,0:T(8,128)(2,1)}, u32[]{:S(2)}) copy-start(bf16[1,3,3,256,256]{4,3,2,1,0:T(8,128)(2,1)} %w_old.3) | copy-start | bytes 3538948
  20.1 18.3 %collective-permute-start.3 = (bf16[11,128,256]{2,1,0:T(8,128)(2,1)S(1)}, bf16[11,128,256]{2,1,0:T(8,128)(2,1)S(1)}, u32[]{:S(2)}, u32[]{:S(2)}) collective-permute-start(bf16[11,128,256]{2,1,0:T(8,128)(2,1)S(1)} %get-tuple-element.25), channel_id=1, source_target_pairs={{0,1},{1,0},{2,3},{3,2},{4,5},{5,4},{6,7},{7,6},{8,9},{9,8},{10,11... | collective-permute-start | bytes 2162696 | tf_op jit(solution)/shard_map/ppermute | solution.py:487
  23.0 27.9 %collective-permute-start.1 = (bf16[9,128,256]{2,1,0:T(8,128)(2,1)S(1)}, bf16[9,128,256]{2,1,0:T(8,128)(2,1)S(1)}, u32[]{:S(2)}, u32[]{:S(2)}) collective-permute-start(bf16[9,128,256]{2,1,0:T(8,128)(2,1)S(1)} %shard_map.129), channel_id=1, source_target_pairs={{0,2},{2,4},{4,6},{6,8},{8,10},{10,12},{12,14},{14,16},{16,18},{18... | collective-permute-start | bytes 1769480 | tf_op jit(solution)/shard_map/ppermute | solution.py:29
  24.4 12.1 %collective-permute-start.8 = (bf16[4,128,256]{2,1,0:T(8,128)(2,1)S(1)}, bf16[4,128,256]{2,1,0:T(8,128)(2,1)S(1)}, u32[]{:S(2)}, u32[]{:S(2)}) collective-permute-start(bf16[4,128,256]{2,1,0:T(8,128)(2,1)S(1)} %pad_maximum_fusion.1), channel_id=1, source_target_pairs={{22,30},{23,31}} | collective-permute-start | bytes 786440 | tf_op jit(solution)/shard_map/ppermute | solution.py:464
  31.5 23.3 %collective-permute-start.5 = (bf16[9,128,256]{2,1,0:T(8,128)(2,1)S(1)}, bf16[9,128,256]{2,1,0:T(8,128)(2,1)S(1)}, u32[]{:S(2)}, u32[]{:S(2)}) collective-permute-start(bf16[9,128,256]{2,1,0:T(8,128)(2,1)S(1)} %get-tuple-element.32), channel_id=1, source_target_pairs={{2,0},{4,2},{6,4},{8,6},{10,8},{12,10},{14,12},{16,14},{18,16},{20... | collective-permute-start | bytes 1769480 | tf_op jit(solution)/shard_map/ppermute | solution.py:29
  35.1 19.6 %collective-permute-start.4 = (bf16[2,128,256]{2,1,0:T(8,128)(2,1)S(1)}, bf16[2,128,256]{2,1,0:T(8,128)(2,1)S(1)}, u32[]{:S(2)}, u32[]{:S(2)}) collective-permute-start(bf16[2,128,256]{2,1,0:T(8,128)(2,1)S(1)} %get-tuple-element.31), channel_id=1, source_target_pairs={{0,1},{1,0},{2,3},{3,2},{4,5},{5,4},{6,7},{7,6},{8,9},{9,8},{10,11... | collective-permute-start | bytes 393224 | tf_op jit(solution)/shard_map/ppermute | solution.py:487
  36.4 23.4 %collective-permute-start.9 = (bf16[6,128,256]{2,1,0:T(8,128)(2,1)S(1)}, bf16[6,128,256]{2,1,0:T(8,128)(2,1)S(1)}, u32[]{:S(2)}, u32[]{:S(2)}) collective-permute-start(bf16[6,128,256]{2,1,0:T(8,128)(2,1)S(1)} %get-tuple-element.34), channel_id=1, source_target_pairs={{0,1},{1,0},{2,3},{3,2},{4,5},{5,4},{6,7},{7,6},{8,9},{9,8},{10,11... | collective-permute-start | bytes 1179656 | tf_op jit(solution)/shard_map/ppermute | solution.py:487
  38.3 9.8 %copy-start.5 = (f32[1,3,3,256,256]{4,3,2,1,0:T(8,128)S(1)}, f32[1,3,3,256,256]{4,3,2,1,0:T(8,128)}, u32[]{:S(2)}) copy-start(f32[1,3,3,256,256]{4,3,2,1,0:T(8,128)} %moment.1) | copy-start | bytes 7077892
  41.6 18.2 %collective-permute-start.10 = (bf16[7,128,256]{2,1,0:T(8,128)(2,1)S(1)}, bf16[7,128,256]{2,1,0:T(8,128)(2,1)S(1)}, u32[]{:S(2)}, u32[]{:S(2)}) collective-permute-start(bf16[7,128,256]{2,1,0:T(8,128)(2,1)S(1)} %get-tuple-element.36), channel_id=1, source_target_pairs={{2,0},{4,2},{6,4},{8,6},{10,8},{12,10},{14,12},{16,14},{18,16},{20... | collective-permute-start | bytes 1376264 | tf_op jit(solution)/shard_map/ppermute | solution.py:29
  48.1 2.8 %copy-start.11 = (bf16[8,128,256]{2,1,0:T(8,128)(2,1)S(1)}, bf16[8,128,256]{2,1,0:T(8,128)(2,1)}, u32[]{:S(2)}) copy-start(bf16[8,128,256]{2,1,0:T(8,128)(2,1)} %next_in.3) | copy-start | bytes 1572868
  48.1 6.6 %copy-start.13 = (bf16[8,128,256]{2,1,0:T(8,128)(2,1)S(1)}, bf16[8,128,256]{2,1,0:T(8,128)(2,1)}, u32[]{:S(2)}) copy-start(bf16[8,128,256]{2,1,0:T(8,128)(2,1)} %next_g.3) | copy-start | bytes 1572868
  51.0 1.3 %copy-start.8 = (bf16[1,3,3,256,256]{4,3,2,1,0:T(8,128)(2,1)S(1)}, bf16[1,3,3,256,256]{4,3,2,1,0:T(8,128)(2,1)}, u32[]{:S(2)}) copy-start(bf16[1,3,3,256,256]{4,3,2,1,0:T(8,128)(2,1)} %get-tuple-element.21.w_one) | copy-start | bytes 3538948
  54.8 5.1 %copy-start.9 = (bf16[1,3,3,256,256]{4,3,2,1,0:T(8,128)(2,1)S(1)}, bf16[1,3,3,256,256]{4,3,2,1,0:T(8,128)(2,1)}, u32[]{:S(2)}) copy-start(bf16[1,3,3,256,256]{4,3,2,1,0:T(8,128)(2,1)} %get-tuple-element.21.w_one) | copy-start | bytes 3538948
  (2 other events, 2.1 us)
